TPU v7x, 256 devices: a whole 4x4x8 slice. The times are simulated.
256 devices in a mesh: dp: 4 (over y), seq: 64 (over z, x, core).
Axes of the slice: x: 4, y: 4, z: 8, core: 2. Of those that a mesh axis runs over, the one named last changes fastest.
Arguments:
- query: bfloat16 [4, 16384, 1536], P('dp', 'seq'), may hold values from -6 to 6
- key: bfloat16 [4, 16384, 1536], P('dp', 'seq'), may hold values from -6 to 6
- value: bfloat16 [4, 16384, 1536], P('dp', 'seq'), may hold values from -6 to 6
- segments: int32 [4, 16384], P('dp', 'seq'), may hold values from 0 to 95, never falling along the last dimension, each value on 1 to 256 neighbouring positions
- out_proj: bfloat16 [1536, 1536], replicated, may hold values from -0.15625 to 0.15625
- conv_kernel: bfloat16 [31, 1536], replicated, may hold values from -1 to 1
- cotangent: bfloat16 [4, 16384, 1536], P('dp', 'seq'), may hold values from -6 to 6
Outputs:
- block_out: bfloat16 [4, 16384, 1536], P('dp', 'seq')
- grad_query: bfloat16 [4, 16384, 1536], P('dp', 'seq')
- grad_key: bfloat16 [4, 16384, 1536], P('dp', 'seq')
- grad_value: bfloat16 [4, 16384, 1536], P('dp', 'seq')
- grad_kernel: float32 [31, 1536], replicated
- grad_out_proj: float32 [1536, 1536], P(('dp', 'seq'))
Inputs may be any that keep to these rules, and one draw needn't show every extreme that they name: `segments`: along the frames of a data group the utterance number never falls; every utterance holds 1 to 256 frames and one holds exactly 256.
All inputs are finite; a program needn't handle non-finite values.
Results may differ from a plain program's by a relative error of at most 0.02.
Values may be sent and summed in bfloat16 or wider, within the bound.
No kernel may reach another device: no remote copies, remote signals or barrier semaphores. Data moves between devices by JAX's collectives and lax.ppermute only.
A program may use at most 128 MiB of HBM per device.

v0:
```python
import jax
import jax.numpy as jnp
from jax import lax
from jax.sharding import PartitionSpec as P

HD = 64
KW = 31


def extended(block, sides, width):
    for axis, dim in sides:
        count = lax.axis_size(axis)
        forward = [(i, i + 1) for i in range(count - 1)]
        backward = [(target, source) for source, target in forward]
        low = lax.ppermute(
            lax.slice_in_dim(block, block.shape[dim] - width, None, axis=dim), axis, forward
        )
        high = lax.ppermute(lax.slice_in_dim(block, 0, width, axis=dim), axis, backward)
        block = jnp.concatenate([low, block, high], axis=dim)
    return block


def from_behind(value, axis, steps):
    count = lax.axis_size(axis)
    first, last = (max(0, -steps), min(count, count - steps))
    return lax.ppermute(value, axis, [(source, source + steps) for source in range(first, last)])


def head_scores(queries, keys_block, query_ids, key_ids):
    query_heads = queries.reshape(queries.shape[0], -1, HD)
    key_heads = keys_block.reshape(keys_block.shape[0], -1, HD)
    scores = jnp.einsum(
        "rhe,whe->hrw", query_heads, key_heads, preferred_element_type=jnp.float32
    ) * HD ** (-0.5)
    allowed = query_ids[:, None] == key_ids[None, :]
    return jnp.where(allowed[None], scores, -1e30)


def to_groups(matrix):
    return jnp.moveaxis(matrix.reshape(matrix.shape[0], -1, 4 * HD), 1, 0)


def from_groups(stacked):
    return jnp.moveaxis(stacked, 0, 1).reshape(stacked.shape[1], -1)


def attend(queries, keys_block, values_block, query_ids, key_ids):
    scores = head_scores(queries, keys_block, query_ids, key_ids)
    highest = jnp.max(scores, axis=2)
    weights = jnp.exp(scores - highest[:, :, None])
    totals = jnp.sum(weights, axis=2)
    probs = (weights / totals[:, :, None]).astype(jnp.bfloat16)
    value_heads = values_block.reshape(values_block.shape[0], -1, HD)
    context = jnp.einsum("hrw,whe->rhe", probs, value_heads, preferred_element_type=jnp.float32)
    return (context.reshape(queries.shape[0], -1), highest, totals)


def score_grads(
    queries, keys_block, values_block, upstream, highest, totals, deltas, query_ids, key_ids
):
    scores = head_scores(queries, keys_block, query_ids, key_ids)
    probs = jnp.exp(scores - highest[:, :, None]) / totals[:, :, None]
    upstream_heads = upstream.reshape(upstream.shape[0], -1, HD)
    value_heads = values_block.reshape(values_block.shape[0], -1, HD)
    prob_grads = jnp.einsum(
        "rhe,whe->hrw", upstream_heads, value_heads, preferred_element_type=jnp.float32
    )
    score_grad = (probs * (prob_grads - deltas[:, :, None]) * HD ** (-0.5)).astype(jnp.bfloat16)
    return (probs.astype(jnp.bfloat16), score_grad, upstream_heads)


def query_side(queries, keys_block, score_grad):
    key_heads = keys_block.reshape(keys_block.shape[0], -1, HD)
    grads = jnp.einsum("hrw,whe->rhe", score_grad, key_heads, preferred_element_type=jnp.float32)
    return grads.reshape(queries.shape[0], -1)


def key_side(queries, keys_block, probs, score_grad, upstream_heads):
    query_heads = queries.reshape(queries.shape[0], -1, HD)
    key_part = jnp.einsum(
        "hrw,rhe->whe", score_grad, query_heads, preferred_element_type=jnp.float32
    )
    value_part = jnp.einsum(
        "hrw,rhe->whe", probs, upstream_heads, preferred_element_type=jnp.float32
    )
    return (key_part.reshape(keys_block.shape[0], -1), value_part.reshape(keys_block.shape[0], -1))


def per_device(query, key, value, segments, out_proj, conv_kernel, cotangent):
    frame_count = query.shape[1]
    width = query.shape[2]
    group_count = width // (4 * HD)
    reach = KW // 2
    queries = query[0]
    keys_local = key[0]
    values_local = value[0]
    own_ids = segments[0] + 1
    wide_ids = extended(own_ids, (("seq", 0),), frame_count)
    paired = extended(jnp.stack([keys_local, values_local]), (("seq", 1),), frame_count)

    def forward_group(items):
        return attend(items[0], items[1], items[2], own_ids, wide_ids)

    context_groups, highest, totals = lax.map(
        forward_group, (to_groups(queries), to_groups(paired[0]), to_groups(paired[1]))
    )
    context = from_groups(context_groups)
    context_b = context.astype(jnp.bfloat16)
    attended = jnp.dot(context_b, out_proj, preferred_element_type=jnp.float32).astype(jnp.bfloat16)
    attended_wide = extended(attended, (("seq", 0),), reach)
    conv_ids = wide_ids[frame_count - reach : 2 * frame_count + reach]
    kernel = conv_kernel.astype(jnp.float32)
    masks = [(conv_ids[offset : offset + frame_count] == own_ids)[:, None] for offset in range(KW)]
    convolved = jnp.zeros((frame_count, width), jnp.float32)
    for offset in range(KW):
        convolved = convolved + jnp.where(
            masks[offset],
            kernel[offset] * attended_wide[offset : offset + frame_count].astype(jnp.float32),
            0.0,
        )
    gate = jax.nn.sigmoid(convolved)
    block_out = (convolved * gate).astype(jnp.bfloat16)
    conv_grad = (cotangent[0].astype(jnp.float32) * gate * (1.0 + convolved * (1.0 - gate))).astype(
        jnp.bfloat16
    )
    conv_grad_wide = extended(conv_grad, (("seq", 0),), reach)
    conv_grad_f = conv_grad.astype(jnp.float32)
    attended_grad = jnp.zeros((frame_count, width), jnp.float32)
    kernel_rows = []
    for offset in range(KW):
        mirror = 2 * reach - offset
        attended_grad = attended_grad + jnp.where(
            masks[mirror],
            kernel[offset] * conv_grad_wide[mirror : mirror + frame_count].astype(jnp.float32),
            0.0,
        )
        kernel_rows.append(
            jnp.sum(
                jnp.where(
                    masks[offset],
                    conv_grad_f * attended_wide[offset : offset + frame_count].astype(jnp.float32),
                    0.0,
                ),
                axis=0,
            )
        )
    scale_out = (lax.axis_size("dp") * lax.axis_size("seq") * frame_count) ** (-0.5)
    grad_kernel = lax.psum(jnp.stack(kernel_rows), ("dp", "seq")) * scale_out
    attended_grad_b = attended_grad.astype(jnp.bfloat16)
    reduced = lax.psum_scatter(
        lax.dot_general(
            context_b, attended_grad_b, (((0,), (0,)), ((), ())), preferred_element_type=jnp.float32
        ),
        ("dp", "seq"),
        scatter_dimension=0,
        tiled=True,
    )
    grad_out_proj = reduced * scale_out
    context_grad = lax.dot_general(
        attended_grad_b, out_proj, (((1,), (1,)), ((), ())), preferred_element_type=jnp.float32
    ).astype(jnp.bfloat16)
    products = (to_groups(context_grad).astype(jnp.float32) * to_groups(context)).reshape(
        group_count, frame_count, 4, HD
    )
    deltas = jnp.moveaxis(jnp.sum(products, axis=3), 2, 1)

    def both_group(items):
        probs, score_grad, upstream_heads = score_grads(
            items[0], items[1], items[2], items[3], items[4], items[5], items[6], own_ids, wide_ids
        )
        key_part, value_part = key_side(items[0], items[1], probs, score_grad, upstream_heads)
        return (query_side(items[0], items[1], score_grad), key_part, value_part)

    query_part, key_part, value_part = lax.map(
        both_group,
        (
            to_groups(queries),
            to_groups(paired[0]),
            to_groups(paired[1]),
            to_groups(context_grad),
            highest,
            totals,
            deltas,
        ),
    )
    key_wide = from_groups(key_part)
    value_wide = from_groups(value_part)
    earlier = jnp.stack([key_wide[:frame_count], value_wide[:frame_count]])
    later = jnp.stack([key_wide[2 * frame_count :], value_wide[2 * frame_count :]])
    from_later = from_behind(earlier.astype(jnp.bfloat16), "seq", -1).astype(earlier.dtype)
    from_earlier = from_behind(later.astype(jnp.bfloat16), "seq", 1).astype(later.dtype)
    key_total = key_wide[frame_count : 2 * frame_count] + from_later[0] + from_earlier[0]
    value_total = value_wide[frame_count : 2 * frame_count] + from_later[1] + from_earlier[1]
    grad_query = from_groups(query_part).astype(jnp.bfloat16)
    grad_key = key_total.astype(jnp.bfloat16)
    grad_value = value_total.astype(jnp.bfloat16)
    return (
        block_out[None],
        grad_query[None],
        grad_key[None],
        grad_value[None],
        grad_kernel,
        grad_out_proj,
    )


def solution(mesh):
    in_specs = (
        P("dp", "seq", None),
        P("dp", "seq", None),
        P("dp", "seq", None),
        P("dp", "seq"),
        P(),
        P(),
        P("dp", "seq", None),
    )
    out_specs = (
        P("dp", "seq", None),
        P("dp", "seq", None),
        P("dp", "seq", None),
        P("dp", "seq", None),
        P(),
        P(("dp", "seq"), None),
    )
    return jax.shard_map(
        per_device, mesh=mesh, in_specs=in_specs, out_specs=out_specs, check_vma=False
    )
```

profile of v0, /device:TPU:1, one launch (start us, length us, event | category | flops | bytes accessed | tf_op | source)
XLA Modules:
  0.0 1732.6 jit_solution(641398557045694055)
XLA Ops:
  8.6 15.1 collective-permute-start.1
  30.7 13.3 collective-permute-start.3
  59.3 38.1 %while.30 = (s32[]{:T(128)}, f32[6,256,256]{1,2,0:T(8,128)}, f32[6,4,256]{2,1,0:T(4,128)}, f32[6,4,256]{2,1,0:T(4,128)}, bf16[6,768,256]{1,2,0:T(8,128)(2,1)S(1)...) while((s32[]{:T(128)}, f32[6,256,256]{1,2,0:T(8,128)}, ...), condition=%wide.region_3.4_spmd.clone, body=%wide.region_0.3_spmd.sunk.clone | while | flops 210958336 | bytes 13804649 | solution.py:104
  112.0 22.7 %fusion.142 = (f32[1536]{0:T(1024)}, f32[1536]{0:T(1024)}, f32[1536]{0:T(1024)}, f32[1536]{0:T(1024)}, f32[1536]{0:T(1024)}, /*index=5*/f32[1536]{0:T(1024)}, bf16[256,1536]{1,0:T(8,128)(2,1)S(1)}, f32[256,1536]{1,0:T(8,128)}) fusion(pred[256]{0:T(512)(128)(4,1)S(1)} %get-tuple-element.289, bf16[15,1536]{1,0:T(8,128)(2,1)S(1)} %collective-permute-done.5, ...), kind=kLoop, calls=%fused_computation.286 | loop fusion | flops 104193024 | bytes 4259328 | tf_op jit(solution)/shard_map/reduce_sum | solution.py:138
  142.5 24.2 %fusion.149 = bf16[256,1536]{1,0:T(8,128)(2,1)S(1)} fusion(bf16[256,1536]{1,0:T(8,128)(2,1)S(1)} %get-tuple-element.248, bf16[15,1536]{1,0:T(8,128)(2,1)} %collective-permute-done.7, bf16[15,1536]{1,0:T(8,128)(2,1)} %copy-done.74, f32[1536]{0:T(1024)S(1)} %get-tuple-element.174, f32[1536]{0:T(1024)S(1)} %get-tuple-element.175, ...), kind=kLoop, calls=%fused_computation.304 | loop fusion | flops 83755008 | bytes 1863168 | tf_op jit(solution)/shard_map/convert_element_type | solution.py:149
  171.8 723.4 %fusion = f32[8,1536]{1,0:T(8,128)S(1)} fusion(f32[1536,1536]{1,0:T(8,128)} %fusion.216), kind=kCustom, calls=%all-reduce-scatter | all-reduce-scatter fusion | flops 3145729 | bytes 9486336
  897.8 13.3 collective-permute-start.11
  930.9 13.1 collective-permute-start.13
  944.0 13.1 collective-permute-start.14
  957.2 13.1 collective-permute-start.15
  970.3 13.1 collective-permute-start.16
  1002.5 13.1 collective-permute-start.18
  1015.7 13.1 collective-permute-start.19
  1028.8 13.1 collective-permute-start.20
  1042.0 13.1 collective-permute-start.21
  1071.9 13.1 collective-permute-start.23
  1085.0 13.1 collective-permute-start.24
  1098.2 13.1 collective-permute-start.25
  1111.3 13.3 collective-permute-start.26
  1128.1 13.1 collective-permute-start.27
  1141.2 13.7 collective-permute-start.28
  1154.9 13.1 collective-permute-start.29
  1168.1 13.1 collective-permute-start.30
  1181.2 13.1 collective-permute-start.31
  1213.2 13.1 collective-permute-start.33
  1226.4 13.1 collective-permute-start.34
  1267.5 13.7 collective-permute-start.37
  1281.2 13.1 collective-permute-start.38
  1294.4 13.1 collective-permute-start.39
  1318.2 52.4 %while.31 = (s32[]{:T(128)}, bf16[6,256,256]{1,2,0:T(8,128)(2,1)S(1)}, f32[6,768,256]{1,2,0:T(8,128)}, f32[6,768,256]{1,2,0:T(8,128)}, bf16[6,768,256]{1,2,0:T(8...) while((s32[]{:T(128)}, ...), condition=%wide.region_6.7_spmd.clone, body=%wide.region_5.6_spmd.sunk.clone | while | flops 510590976 | bytes 23504016 | solution.py:174
  1489.9 96.9 %concatenate.118 = f32[518,1536]{1,0:T(8,128)} concatenate(f32[6,1536]{1,0:T(8,128)S(1)} %collective-permute-done.73, f32[8,1536]{1,0:T(8,128)} %collective-permute-done.72, f32[8,1536]{1,0:T(8,128)} %collective-permute-done.71, f32[8,1536]{1,0:T(8,128)} %collective-permute-done.70, f32[8,1536]{1,0:T(8,128)} %collective-permute-done.69, f32[8,1536]{1,0:T(8,128)} %collective-permute-done.68, ...), dimensions={0} | concatenate | bytes 6365184
  1588.4 128.7 %all-reduce.4.cloned.1.call-done = f32[31,1536]{1,0:T(8,128)} async-done(((f32[31,1536]{1,0:T(8,128)}), f32[31,1536]{1,0:T(8,128)}) %all-reduce.4.cloned.1.call-update) | async-done | bytes 190480 | tf_op jit(solution)/shard_map/psum | solution.py:148
  (656 shorter events, 386.5 us)
Async XLA Ops:
  7.2 1709.9 %all-reduce.4.cloned.1.call-start = ((), (), s32[]{:S(2)}) async-start(), calls=%async_computation | async-start | bytes 393216 | tf_op jit(solution)/shard_map/psum | solution.py:148
  897.8 72.5 %collective-permute-start.11 = (f32[8,1536]{1,0:T(8,128)S(1)}, f32[8,1536]{1,0:T(8,128)S(1)}, u32[]{:S(2)}, u32[]{:S(2)}) collective-permute-start(f32[8,1536]{1,0:T(8,128)S(1)} %fusion), channel_id=1, source_target_pairs={{0,2},{1,3},{2,4},{3,5},{4,6},{5,7},{6,8},{7,9},{8,10},{9,11},{10,... | collective-permute-start | bytes 147464
  917.8 71.6 %collective-permute-start.12 = (f32[8,1536]{1,0:T(8,128)S(1)}, f32[8,1536]{1,0:T(8,128)S(1)}, u32[]{:S(2)}, u32[]{:S(2)}) collective-permute-start(f32[8,1536]{1,0:T(8,128)S(1)} %fusion), channel_id=1, source_target_pairs={{0,3},{1,4},{2,5},{3,6},{4,7},{5,8},{6,9},{7,10},{8,11},{9,12},{10... | collective-permute-start | bytes 147464
  930.9 71.6 %collective-permute-start.13 = (f32[8,1536]{1,0:T(8,128)S(1)}, f32[8,1536]{1,0:T(8,128)S(1)}, u32[]{:S(2)}, u32[]{:S(2)}) collective-permute-start(f32[8,1536]{1,0:T(8,128)S(1)} %fusion), channel_id=1, source_target_pairs={{0,4},{1,5},{2,6},{3,7},{4,8},{5,9},{6,10},{7,11},{8,12},{9,13},{1... | collective-permute-start | bytes 147464
  944.0 71.6 %collective-permute-start.14 = (f32[8,1536]{1,0:T(8,128)S(1)}, f32[8,1536]{1,0:T(8,128)S(1)}, u32[]{:S(2)}, u32[]{:S(2)}) collective-permute-start(f32[8,1536]{1,0:T(8,128)S(1)} %fusion), channel_id=1, source_target_pairs={{0,5},{1,6},{2,7},{3,8},{4,9},{5,10},{6,11},{7,12},{8,13},{9,14},{... | collective-permute-start | bytes 147464
  957.2 71.7 %collective-permute-start.15 = (f32[8,1536]{1,0:T(8,128)S(1)}, f32[8,1536]{1,0:T(8,128)S(1)}, u32[]{:S(2)}, u32[]{:S(2)}) collective-permute-start(f32[8,1536]{1,0:T(8,128)S(1)} %fusion), channel_id=1, source_target_pairs={{0,6},{1,7},{2,8},{3,9},{4,10},{5,11},{6,12},{7,13},{8,14},{9,15},... | collective-permute-start | bytes 147464
  970.3 71.7 %collective-permute-start.16 = (f32[8,1536]{1,0:T(8,128)S(1)}, f32[8,1536]{1,0:T(8,128)S(1)}, u32[]{:S(2)}, u32[]{:S(2)}) collective-permute-start(f32[8,1536]{1,0:T(8,128)S(1)} %fusion), channel_id=1, source_target_pairs={{0,7},{1,8},{2,9},{3,10},{4,11},{5,12},{6,13},{7,14},{8,15},{9,16}... | collective-permute-start | bytes 147464
  989.4 69.4 %collective-permute-start.17 = (f32[8,1536]{1,0:T(8,128)S(1)}, f32[8,1536]{1,0:T(8,128)S(1)}, u32[]{:S(2)}, u32[]{:S(2)}) collective-permute-start(f32[8,1536]{1,0:T(8,128)S(1)} %fusion), channel_id=1, source_target_pairs={{0,8},{1,9},{2,10},{3,11},{4,12},{5,13},{6,14},{7,15},{8,16},{9,17... | collective-permute-start | bytes 147464
  1002.5 69.3 %collective-permute-start.18 = (f32[8,1536]{1,0:T(8,128)S(1)}, f32[8,1536]{1,0:T(8,128)S(1)}, u32[]{:S(2)}, u32[]{:S(2)}) collective-permute-start(f32[8,1536]{1,0:T(8,128)S(1)} %fusion), channel_id=1, source_target_pairs={{0,9},{1,10},{2,11},{3,12},{4,13},{5,14},{6,15},{7,16},{8,17},{9,1... | collective-permute-start | bytes 147464
  1015.7 69.3 %collective-permute-start.19 = (f32[8,1536]{1,0:T(8,128)S(1)}, f32[8,1536]{1,0:T(8,128)S(1)}, u32[]{:S(2)}, u32[]{:S(2)}) collective-permute-start(f32[8,1536]{1,0:T(8,128)S(1)} %fusion), channel_id=1, source_target_pairs={{0,10},{1,11},{2,12},{3,13},{4,14},{5,15},{6,16},{7,17},{8,18},{9,... | collective-permute-start | bytes 147464
  1028.8 69.3 %collective-permute-start.20 = (f32[8,1536]{1,0:T(8,128)S(1)}, f32[8,1536]{1,0:T(8,128)S(1)}, u32[]{:S(2)}, u32[]{:S(2)}) collective-permute-start(f32[8,1536]{1,0:T(8,128)S(1)} %fusion), channel_id=1, source_target_pairs={{0,11},{1,12},{2,13},{3,14},{4,15},{5,16},{6,17},{7,18},{8,19},{9,... | collective-permute-start | bytes 147464
  1042.0 69.3 %collective-permute-start.21 = (f32[8,1536]{1,0:T(8,128)S(1)}, f32[8,1536]{1,0:T(8,128)S(1)}, u32[]{:S(2)}, u32[]{:S(2)}) collective-permute-start(f32[8,1536]{1,0:T(8,128)S(1)} %fusion), channel_id=1, source_target_pairs={{0,12},{1,13},{2,14},{3,15},{4,16},{5,17},{6,18},{7,19},{8,20},{9,... | collective-permute-start | bytes 147464
  1058.8 69.3 %collective-permute-start.22 = (f32[8,1536]{1,0:T(8,128)S(1)}, f32[8,1536]{1,0:T(8,128)S(1)}, u32[]{:S(2)}, u32[]{:S(2)}) collective-permute-start(f32[8,1536]{1,0:T(8,128)S(1)} %fusion), channel_id=1, source_target_pairs={{0,13},{1,14},{2,15},{3,16},{4,17},{5,18},{6,19},{7,20},{8,21},{9,... | collective-permute-start | bytes 147464
  1071.9 69.3 %collective-permute-start.23 = (f32[8,1536]{1,0:T(8,128)S(1)}, f32[8,1536]{1,0:T(8,128)S(1)}, u32[]{:S(2)}, u32[]{:S(2)}) collective-permute-start(f32[8,1536]{1,0:T(8,128)S(1)} %fusion), channel_id=1, source_target_pairs={{0,14},{1,15},{2,16},{3,17},{4,18},{5,19},{6,20},{7,21},{8,22},{9,... | collective-permute-start | bytes 147464
  1085.0 69.9 %collective-permute-start.24 = (f32[8,1536]{1,0:T(8,128)S(1)}, f32[8,1536]{1,0:T(8,128)S(1)}, u32[]{:S(2)}, u32[]{:S(2)}) collective-permute-start(f32[8,1536]{1,0:T(8,128)S(1)} %fusion), channel_id=1, source_target_pairs={{0,15},{1,16},{2,17},{3,18},{4,19},{5,20},{6,21},{7,22},{8,23},{9,... | collective-permute-start | bytes 147464
  1098.2 69.9 %collective-permute-start.25 = (f32[8,1536]{1,0:T(8,128)S(1)}, f32[8,1536]{1,0:T(8,128)S(1)}, u32[]{:S(2)}, u32[]{:S(2)}) collective-permute-start(f32[8,1536]{1,0:T(8,128)S(1)} %fusion), channel_id=1, source_target_pairs={{0,16},{1,17},{2,18},{3,19},{4,20},{5,21},{6,22},{7,23},{8,24},{9,... | collective-permute-start | bytes 147464
  1111.3 69.9 %collective-permute-start.26 = (f32[8,1536]{1,0:T(8,128)S(1)}, f32[8,1536]{1,0:T(8,128)S(1)}, u32[]{:S(2)}, u32[]{:S(2)}) collective-permute-start(f32[8,1536]{1,0:T(8,128)S(1)} %fusion), channel_id=1, source_target_pairs={{0,17},{1,18},{2,19},{3,20},{4,21},{5,22},{6,23},{7,24},{8,25},{9,... | collective-permute-start | bytes 147464
  1128.1 72.5 %collective-permute-start.27 = (f32[8,1536]{1,0:T(8,128)S(1)}, f32[8,1536]{1,0:T(8,128)S(1)}, u32[]{:S(2)}, u32[]{:S(2)}) collective-permute-start(f32[8,1536]{1,0:T(8,128)S(1)} %fusion), channel_id=1, source_target_pairs={{0,18},{1,19},{2,20},{3,21},{4,22},{5,23},{6,24},{7,25},{8,26},{9,... | collective-permute-start | bytes 147464
  1141.2 72.0 %collective-permute-start.28 = (f32[8,1536]{1,0:T(8,128)S(1)}, f32[8,1536]{1,0:T(8,128)}, u32[]{:S(2)}, u32[]{:S(2)}) collective-permute-start(f32[8,1536]{1,0:T(8,128)S(1)} %fusion), channel_id=1, source_target_pairs={{0,19},{1,20},{2,21},{3,22},{4,23},{5,24},{6,25},{7,26},{8,27},{9,... | collective-permute-start | bytes 147464
  1154.9 71.4 %collective-permute-start.29 = (f32[8,1536]{1,0:T(8,128)S(1)}, f32[8,1536]{1,0:T(8,128)}, u32[]{:S(2)}, u32[]{:S(2)}) collective-permute-start(f32[8,1536]{1,0:T(8,128)S(1)} %fusion), channel_id=1, source_target_pairs={{0,20},{1,21},{2,22},{3,23},{4,24},{5,25},{6,26},{7,27},{8,28},{9,... | collective-permute-start | bytes 147464
  1168.1 71.4 %collective-permute-start.30 = (f32[8,1536]{1,0:T(8,128)S(1)}, f32[8,1536]{1,0:T(8,128)}, u32[]{:S(2)}, u32[]{:S(2)}) collective-permute-start(f32[8,1536]{1,0:T(8,128)S(1)} %fusion), channel_id=1, source_target_pairs={{0,21},{1,22},{2,23},{3,24},{4,25},{5,26},{6,27},{7,28},{8,29},{9,... | collective-permute-start | bytes 147464
  1181.2 71.4 %collective-permute-start.31 = (f32[8,1536]{1,0:T(8,128)S(1)}, f32[8,1536]{1,0:T(8,128)}, u32[]{:S(2)}, u32[]{:S(2)}) collective-permute-start(f32[8,1536]{1,0:T(8,128)S(1)} %fusion), channel_id=1, source_target_pairs={{0,22},{1,23},{2,24},{3,25},{4,26},{5,27},{6,28},{7,29},{8,30},{9,... | collective-permute-start | bytes 147464
  1213.2 68.0 %collective-permute-start.33 = (f32[8,1536]{1,0:T(8,128)S(1)}, f32[8,1536]{1,0:T(8,128)S(1)}, u32[]{:S(2)}, u32[]{:S(2)}) collective-permute-start(f32[8,1536]{1,0:T(8,128)S(1)} %fusion), channel_id=1, source_target_pairs={{0,24},{1,25},{2,26},{3,27},{4,28},{5,29},{6,30},{7,31},{8,32},{9,... | collective-permute-start | bytes 147464
  1226.4 68.0 %collective-permute-start.34 = (f32[8,1536]{1,0:T(8,128)S(1)}, f32[8,1536]{1,0:T(8,128)S(1)}, u32[]{:S(2)}, u32[]{:S(2)}) collective-permute-start(f32[8,1536]{1,0:T(8,128)S(1)} %fusion), channel_id=1, source_target_pairs={{0,25},{1,26},{2,27},{3,28},{4,29},{5,30},{6,31},{7,32},{8,33},{9,... | collective-permute-start | bytes 147464
  1239.5 68.0 %collective-permute-start.35 = (f32[8,1536]{1,0:T(8,128)S(1)}, f32[8,1536]{1,0:T(8,128)S(1)}, u32[]{:S(2)}, u32[]{:S(2)}) collective-permute-start(f32[8,1536]{1,0:T(8,128)S(1)} %fusion), channel_id=1, source_target_pairs={{0,26},{1,27},{2,28},{3,29},{4,30},{5,31},{6,32},{7,33},{8,34},{9,... | collective-permute-start | bytes 147464
  1267.5 103.1 %collective-permute-start.37 = (f32[8,1536]{1,0:T(8,128)S(1)}, f32[8,1536]{1,0:T(8,128)}, u32[]{:S(2)}, u32[]{:S(2)}) collective-permute-start(f32[8,1536]{1,0:T(8,128)S(1)} %fusion), channel_id=1, source_target_pairs={{0,28},{1,29},{2,30},{3,31},{4,32},{5,33},{6,34},{7,35},{8,36},{9,... | collective-permute-start | bytes 147464
  1281.2 98.0 %collective-permute-start.38 = (f32[8,1536]{1,0:T(8,128)S(1)}, f32[8,1536]{1,0:T(8,128)}, u32[]{:S(2)}, u32[]{:S(2)}) collective-permute-start(f32[8,1536]{1,0:T(8,128)S(1)} %fusion), channel_id=1, source_target_pairs={{0,29},{1,30},{2,31},{3,32},{4,33},{5,34},{6,35},{7,36},{8,37},{9,... | collective-permute-start | bytes 147464
  1294.4 87.9 %collective-permute-start.39 = (f32[8,1536]{1,0:T(8,128)S(1)}, f32[8,1536]{1,0:T(8,128)}, u32[]{:S(2)}, u32[]{:S(2)}) collective-permute-start(f32[8,1536]{1,0:T(8,128)S(1)} %fusion), channel_id=1, source_target_pairs={{0,30},{1,31},{2,32},{3,33},{4,34},{5,35},{6,36},{7,37},{8,38},{9,... | collective-permute-start | bytes 147464
  1307.5 84.3 %collective-permute-start.40 = (f32[8,1536]{1,0:T(8,128)S(1)}, f32[8,1536]{1,0:T(8,128)}, u32[]{:S(2)}, u32[]{:S(2)}) collective-permute-start(f32[8,1536]{1,0:T(8,128)S(1)} %fusion), channel_id=1, source_target_pairs={{0,31},{1,32},{2,33},{3,34},{4,35},{5,36},{6,37},{7,38},{8,39},{9,... | collective-permute-start | bytes 147464
  1315.9 78.8 %collective-permute-start.41 = (f32[8,1536]{1,0:T(8,128)S(1)}, f32[8,1536]{1,0:T(8,128)}, u32[]{:S(2)}, u32[]{:S(2)}) collective-permute-start(f32[8,1536]{1,0:T(8,128)S(1)} %fusion), channel_id=1, source_target_pairs={{0,32},{1,33},{2,34},{3,35},{4,36},{5,37},{6,38},{7,39},{8,40},{9,... | collective-permute-start | bytes 147464
  1466.4 252.4 %collective-permute-start.8 = (bf16[2,256,1536]{1,2,0:T(8,128)(2,1)}, bf16[2,256,1536]{1,2,0:T(8,128)(2,1)}, u32[]{:S(2)}, u32[]{:S(2)}) collective-permute-start(bf16[2,256,1536]{1,2,0:T(8,128)(2,1)} %pad_maximum_fusion.1), channel_id=1, source_target_pairs={{1,0},{2,1},{3,2},{4,3},{5,4},{6,5},{7,6},{8,7},{9,8},{10,9},{11,1... | collective-permute-start | bytes 4718600 | tf_op jit(solution)/shard_map/ppermute | solution.py:26
  1469.0 251.5 %collective-permute-start.9 = (bf16[2,256,1536]{1,2,0:T(8,128)(2,1)}, bf16[2,256,1536]{1,2,0:T(8,128)(2,1)}, u32[]{:S(2)}, u32[]{:S(2)}) collective-permute-start(bf16[2,256,1536]{1,2,0:T(8,128)(2,1)} %pad_maximum_fusion.2), channel_id=1, source_target_pairs={{0,1},{1,2},{2,3},{3,4},{4,5},{5,6},{6,7},{7,8},{8,9},{9,10},{10,1... | collective-permute-start | bytes 4718600 | tf_op jit(solution)/shard_map/ppermute | solution.py:26
  (201 other events, 10669.8 us)
Sparse Core Ops, SparseCore 0:
  1476.9 240.1 all-reduce.3
where the time goes:
time: 1750 us; the launch traced here: 1730 us
  blocking collectives  723 us (41%)
  starting transfers between devices  543 us (31%)
  local copies, waits for them, and re-layouts  176 us (10%)
  waiting for transfers between devices  133 us (8%)
  other arithmetic  95.4 us (5%)
  matrix products  43.9 us (3%)
  between operations  17.7 us (1%)
    unnamed x1, blocking collectives  723 us
    unnamed x64, starting transfers between devices  491 us
    psum x1, waiting for transfers between devices, per_device(): grad_kernel = lax.psum(jnp.stack(kernel_rows), ('dp', 'seq')) * scale_out  129 us
    unnamed x323, local copies, waits for them, and re-layouts  104 us
    reduce_sum x6, other arithmetic, per_device(): jnp.sum(jnp.where(masks[offset], conv_grad_f * attended_wide[offset:offse...  40.2 us
  transfers between devices with their start and end apart: 75, of which 3 were waited for; matrix products, arithmetic and copies ran while one was open for 11% of the time, Pallas kernels for 0%

commit v1 on v0

--- a/solution.py
+++ b/solution.py
@@ -5,6 +5,11 @@
 
 HD = 64
 KW = 31
+
+
+def axis_by_axis(value_2, inner_axis, outer_axis):
+    partial = lax.psum(value_2, inner_axis)
+    return lax.psum(partial, outer_axis)
 
 
 def extended(block, sides, width):
@@ -145,7 +150,7 @@
             )
         )
     scale_out = (lax.axis_size("dp") * lax.axis_size("seq") * frame_count) ** (-0.5)
-    grad_kernel = lax.psum(jnp.stack(kernel_rows), ("dp", "seq")) * scale_out
+    grad_kernel = axis_by_axis(jnp.stack(kernel_rows), "seq", "dp") * scale_out
     attended_grad_b = attended_grad.astype(jnp.bfloat16)
     reduced = lax.psum_scatter(
         lax.dot_general(

time: 1750 us -> 1780 us (1.017)
  waiting for transfers between devices: 133 us -> 162 us
    psum x1 -> x2, waiting for transfers between devices: 129 us -> 158 us  [the longest x1 158 us: axis_by_axis(): partial = lax.psum(value_2, inner_axis)]
    unnamed x323 -> x287, local copies, waits for them, and re-layouts: 104 us -> 109 us
  transfers between devices with their start and end apart: 75 -> 76, of which waited for: 3 -> 2; matrix products, arithmetic and copies ran while one was open for 11% -> 11% of each run, Pallas kernels for 0% -> 0%
where the time goes in v1:
time: 1780 us; the launch traced here: 1770 us
  blocking collectives  723 us (41%)
  starting transfers between devices  544 us (31%)
  local copies, waits for them, and re-layouts  183 us (10%)
  waiting for transfers between devices  162 us (9%)
  other arithmetic  94.3 us (5%)
  matrix products  44.3 us (2%)
    unnamed x1, blocking collectives  723 us
    unnamed x64, starting transfers between devices  491 us
    psum x1, waiting for transfers between devices, axis_by_axis(): partial = lax.psum(value_2, inner_axis)  158 us
    unnamed x287, local copies, waits for them, and re-layouts  109 us
    reduce_sum x6, other arithmetic, per_device(): jnp.sum(jnp.where(masks[offset], conv_grad_f * attended_wide[offset:offse...  40.1 us
  transfers between devices with their start and end apart: 76, of which 2 were waited for; matrix products, arithmetic and copies ran while one was open for 11% of the time, Pallas kernels for 0%

profile of v1, /device:TPU:1, one launch (start us, length us, event | category | flops | bytes accessed | tf_op | source)
XLA Modules:
  0.0 1768.2 jit_solution(8348227823383084855)
XLA Ops:
  8.6 15.1 collective-permute-start.1
  30.7 13.3 collective-permute-start.3
  60.6 40.0 %while.30 = (s32[]{:T(128)}, f32[6,256,256]{1,2,0:T(8,128)S(1)}, f32[6,4,256]{2,1,0:T(4,128)}, f32[6,4,256]{2,1,0:T(4,128)}, bf16[6,768,256]{1,2,0:T(8,128)(2,1)...) while((s32[]{:T(128)}, f32[6,256,256]{1,2,0:T(8,128)S(1)}, ...), condition=%wide.region_3.4_spmd.clone, body=%wide.region_0.3_spmd.sunk.clone | while | flops 210958336 | bytes 13804141 | solution.py:109
  114.4 22.6 %fusion.142 = (f32[1536]{0:T(1024)}, f32[1536]{0:T(1024)}, f32[1536]{0:T(1024)}, f32[1536]{0:T(1024)}, f32[1536]{0:T(1024)}, /*index=5*/f32[1536]{0:T(1024)}, bf16[256,1536]{1,0:T(8,128)(2,1)S(1)}, f32[256,1536]{1,0:T(8,128)}) fusion(pred[256]{0:T(512)(128)(4,1)S(1)} %get-tuple-element.289, bf16[15,1536]{1,0:T(8,128)(2,1)S(1)} %collective-permute-done.5, ...), kind=kLoop, calls=%fused_computation.286 | loop fusion | flops 104193024 | bytes 4259328 | tf_op jit(solution)/shard_map/reduce_sum | solution.py:143
  145.0 24.2 %fusion.149 = bf16[256,1536]{1,0:T(8,128)(2,1)S(1)} fusion(bf16[256,1536]{1,0:T(8,128)(2,1)S(1)} %get-tuple-element.248, bf16[15,1536]{1,0:T(8,128)(2,1)} %collective-permute-done.7, bf16[15,1536]{1,0:T(8,128)(2,1)} %copy-done.56, f32[1536]{0:T(1024)S(1)} %get-tuple-element.174, f32[1536]{0:T(1024)S(1)} %get-tuple-element.175, ...), kind=kLoop, calls=%fused_computation.304 | loop fusion | flops 83755008 | bytes 1863168 | tf_op jit(solution)/shard_map/convert_element_type | solution.py:154
  174.2 723.2 %fusion = f32[8,1536]{1,0:T(8,128)S(1)} fusion(f32[1536,1536]{1,0:T(8,128)} %fusion.216), kind=kCustom, calls=%all-reduce-scatter | all-reduce-scatter fusion | flops 3145729 | bytes 9486336
  899.9 13.3 collective-permute-start.11
  933.1 13.1 collective-permute-start.13
  946.2 13.1 collective-permute-start.14
  959.3 13.1 collective-permute-start.15
  972.5 13.1 collective-permute-start.16
  1004.7 13.1 collective-permute-start.18
  1017.9 13.1 collective-permute-start.19
  1031.0 13.1 collective-permute-start.20
  1044.2 13.1 collective-permute-start.21
  1074.1 13.1 collective-permute-start.23
  1087.2 13.1 collective-permute-start.24
  1100.4 13.1 collective-permute-start.25
  1114.2 13.3 collective-permute-start.26
  1130.9 13.1 collective-permute-start.27
  1144.0 13.7 collective-permute-start.28
  1157.8 13.2 collective-permute-start.29
  1170.9 13.1 collective-permute-start.30
  1184.7 13.1 collective-permute-start.31
  1216.6 13.1 collective-permute-start.33
  1229.7 13.1 collective-permute-start.34
  1270.8 13.7 collective-permute-start.37
  1284.6 13.2 collective-permute-start.38
  1297.7 13.1 collective-permute-start.39
  1321.5 52.4 %while.31 = (s32[]{:T(128)}, bf16[6,256,256]{1,2,0:T(8,128)(2,1)S(1)}, f32[6,768,256]{1,2,0:T(8,128)}, f32[6,768,256]{1,2,0:T(8,128)}, bf16[6,768,256]{1,2,0:T(8...) while((s32[]{:T(128)}, ...), condition=%wide.region_6.7_spmd.clone, body=%wide.region_5.6_spmd.sunk.clone | while | flops 510590976 | bytes 23504016 | solution.py:179
  1492.9 158.4 %all-reduce.5.cloned.1.call-done = f32[31,1536]{1,0:T(8,128)} async-done(((f32[31,1536]{1,0:T(8,128)}), f32[31,1536]{1,0:T(8,128)}) %all-reduce.5.cloned.1.call-update) | async-done | bytes 190480 | tf_op jit(solution)/shard_map/psum | solution.py:11
  1651.4 97.5 %concatenate.118 = f32[518,1536]{1,0:T(8,128)} concatenate(f32[6,1536]{1,0:T(8,128)S(1)} %collective-permute-done.73, f32[8,1536]{1,0:T(8,128)} %collective-permute-done.72, f32[8,1536]{1,0:T(8,128)} %collective-permute-done.71, f32[8,1536]{1,0:T(8,128)} %collective-permute-done.70, f32[8,1536]{1,0:T(8,128)} %collective-permute-done.69, f32[8,1536]{1,0:T(8,128)} %collective-permute-done.68, ...), dimensions={0} | concatenate | bytes 6365184
  (623 shorter events, 392.4 us)
Async XLA Ops:
  7.2 1644.1 %all-reduce.5.cloned.1.call-start = ((), (), s32[]{:S(2)}) async-start(), calls=%async_computation | async-start | bytes 393216 | tf_op jit(solution)/shard_map/psum | solution.py:11
  899.9 72.5 %collective-permute-start.11 = (f32[8,1536]{1,0:T(8,128)S(1)}, f32[8,1536]{1,0:T(8,128)S(1)}, u32[]{:S(2)}, u32[]{:S(2)}) collective-permute-start(f32[8,1536]{1,0:T(8,128)S(1)} %fusion), channel_id=1, source_target_pairs={{0,2},{1,3},{2,4},{3,5},{4,6},{5,7},{6,8},{7,9},{8,10},{9,11},{10,... | collective-permute-start | bytes 147464
  920.0 71.6 %collective-permute-start.12 = (f32[8,1536]{1,0:T(8,128)S(1)}, f32[8,1536]{1,0:T(8,128)S(1)}, u32[]{:S(2)}, u32[]{:S(2)}) collective-permute-start(f32[8,1536]{1,0:T(8,128)S(1)} %fusion), channel_id=1, source_target_pairs={{0,3},{1,4},{2,5},{3,6},{4,7},{5,8},{6,9},{7,10},{8,11},{9,12},{10... | collective-permute-start | bytes 147464
  933.1 71.7 %collective-permute-start.13 = (f32[8,1536]{1,0:T(8,128)S(1)}, f32[8,1536]{1,0:T(8,128)S(1)}, u32[]{:S(2)}, u32[]{:S(2)}) collective-permute-start(f32[8,1536]{1,0:T(8,128)S(1)} %fusion), channel_id=1, source_target_pairs={{0,4},{1,5},{2,6},{3,7},{4,8},{5,9},{6,10},{7,11},{8,12},{9,13},{1... | collective-permute-start | bytes 147464
  946.2 71.7 %collective-permute-start.14 = (f32[8,1536]{1,0:T(8,128)S(1)}, f32[8,1536]{1,0:T(8,128)S(1)}, u32[]{:S(2)}, u32[]{:S(2)}) collective-permute-start(f32[8,1536]{1,0:T(8,128)S(1)} %fusion), channel_id=1, source_target_pairs={{0,5},{1,6},{2,7},{3,8},{4,9},{5,10},{6,11},{7,12},{8,13},{9,14},{... | collective-permute-start | bytes 147464
  959.3 71.7 %collective-permute-start.15 = (f32[8,1536]{1,0:T(8,128)S(1)}, f32[8,1536]{1,0:T(8,128)S(1)}, u32[]{:S(2)}, u32[]{:S(2)}) collective-permute-start(f32[8,1536]{1,0:T(8,128)S(1)} %fusion), channel_id=1, source_target_pairs={{0,6},{1,7},{2,8},{3,9},{4,10},{5,11},{6,12},{7,13},{8,14},{9,15},... | collective-permute-start | bytes 147464
  972.5 71.7 %collective-permute-start.16 = (f32[8,1536]{1,0:T(8,128)S(1)}, f32[8,1536]{1,0:T(8,128)S(1)}, u32[]{:S(2)}, u32[]{:S(2)}) collective-permute-start(f32[8,1536]{1,0:T(8,128)S(1)} %fusion), channel_id=1, source_target_pairs={{0,7},{1,8},{2,9},{3,10},{4,11},{5,12},{6,13},{7,14},{8,15},{9,16}... | collective-permute-start | bytes 147464
  991.6 69.4 %collective-permute-start.17 = (f32[8,1536]{1,0:T(8,128)S(1)}, f32[8,1536]{1,0:T(8,128)S(1)}, u32[]{:S(2)}, u32[]{:S(2)}) collective-permute-start(f32[8,1536]{1,0:T(8,128)S(1)} %fusion), channel_id=1, source_target_pairs={{0,8},{1,9},{2,10},{3,11},{4,12},{5,13},{6,14},{7,15},{8,16},{9,17... | collective-permute-start | bytes 147464
  1004.7 69.3 %collective-permute-start.18 = (f32[8,1536]{1,0:T(8,128)S(1)}, f32[8,1536]{1,0:T(8,128)S(1)}, u32[]{:S(2)}, u32[]{:S(2)}) collective-permute-start(f32[8,1536]{1,0:T(8,128)S(1)} %fusion), channel_id=1, source_target_pairs={{0,9},{1,10},{2,11},{3,12},{4,13},{5,14},{6,15},{7,16},{8,17},{9,1... | collective-permute-start | bytes 147464
  1017.9 69.3 %collective-permute-start.19 = (f32[8,1536]{1,0:T(8,128)S(1)}, f32[8,1536]{1,0:T(8,128)S(1)}, u32[]{:S(2)}, u32[]{:S(2)}) collective-permute-start(f32[8,1536]{1,0:T(8,128)S(1)} %fusion), channel_id=1, source_target_pairs={{0,10},{1,11},{2,12},{3,13},{4,14},{5,15},{6,16},{7,17},{8,18},{9,... | collective-permute-start | bytes 147464
  1031.0 69.3 %collective-permute-start.20 = (f32[8,1536]{1,0:T(8,128)S(1)}, f32[8,1536]{1,0:T(8,128)S(1)}, u32[]{:S(2)}, u32[]{:S(2)}) collective-permute-start(f32[8,1536]{1,0:T(8,128)S(1)} %fusion), channel_id=1, source_target_pairs={{0,11},{1,12},{2,13},{3,14},{4,15},{5,16},{6,17},{7,18},{8,19},{9,... | collective-permute-start | bytes 147464
  1061.0 69.9 %collective-permute-start.22 = (f32[8,1536]{1,0:T(8,128)S(1)}, f32[8,1536]{1,0:T(8,128)S(1)}, u32[]{:S(2)}, u32[]{:S(2)}) collective-permute-start(f32[8,1536]{1,0:T(8,128)S(1)} %fusion), channel_id=1, source_target_pairs={{0,13},{1,14},{2,15},{3,16},{4,17},{5,18},{6,19},{7,20},{8,21},{9,... | collective-permute-start | bytes 147464
  1074.1 69.9 %collective-permute-start.23 = (f32[8,1536]{1,0:T(8,128)S(1)}, f32[8,1536]{1,0:T(8,128)S(1)}, u32[]{:S(2)}, u32[]{:S(2)}) collective-permute-start(f32[8,1536]{1,0:T(8,128)S(1)} %fusion), channel_id=1, source_target_pairs={{0,14},{1,15},{2,16},{3,17},{4,18},{5,19},{6,20},{7,21},{8,22},{9,... | collective-permute-start | bytes 147464
  1087.2 70.5 %collective-permute-start.24 = (f32[8,1536]{1,0:T(8,128)S(1)}, f32[8,1536]{1,0:T(8,128)S(1)}, u32[]{:S(2)}, u32[]{:S(2)}) collective-permute-start(f32[8,1536]{1,0:T(8,128)S(1)} %fusion), channel_id=1, source_target_pairs={{0,15},{1,16},{2,17},{3,18},{4,19},{5,20},{6,21},{7,22},{8,23},{9,... | collective-permute-start | bytes 147464
  1100.4 70.5 %collective-permute-start.25 = (f32[8,1536]{1,0:T(8,128)S(1)}, f32[8,1536]{1,0:T(8,128)S(1)}, u32[]{:S(2)}, u32[]{:S(2)}) collective-permute-start(f32[8,1536]{1,0:T(8,128)S(1)} %fusion), channel_id=1, source_target_pairs={{0,16},{1,17},{2,18},{3,19},{4,20},{5,21},{6,22},{7,23},{8,24},{9,... | collective-permute-start | bytes 147464
  1114.2 69.9 %collective-permute-start.26 = (f32[8,1536]{1,0:T(8,128)S(1)}, f32[8,1536]{1,0:T(8,128)S(1)}, u32[]{:S(2)}, u32[]{:S(2)}) collective-permute-start(f32[8,1536]{1,0:T(8,128)S(1)} %fusion), channel_id=1, source_target_pairs={{0,17},{1,18},{2,19},{3,20},{4,21},{5,22},{6,23},{7,24},{8,25},{9,... | collective-permute-start | bytes 147464
  1130.9 73.0 %collective-permute-start.27 = (f32[8,1536]{1,0:T(8,128)S(1)}, f32[8,1536]{1,0:T(8,128)S(1)}, u32[]{:S(2)}, u32[]{:S(2)}) collective-permute-start(f32[8,1536]{1,0:T(8,128)S(1)} %fusion), channel_id=1, source_target_pairs={{0,18},{1,19},{2,20},{3,21},{4,22},{5,23},{6,24},{7,25},{8,26},{9,... | collective-permute-start | bytes 147464
  1144.0 72.6 %collective-permute-start.28 = (f32[8,1536]{1,0:T(8,128)S(1)}, f32[8,1536]{1,0:T(8,128)}, u32[]{:S(2)}, u32[]{:S(2)}) collective-permute-start(f32[8,1536]{1,0:T(8,128)S(1)} %fusion), channel_id=1, source_target_pairs={{0,19},{1,20},{2,21},{3,22},{4,23},{5,24},{6,25},{7,26},{8,27},{9,... | collective-permute-start | bytes 147464
  1157.8 72.0 %collective-permute-start.29 = (f32[8,1536]{1,0:T(8,128)S(1)}, f32[8,1536]{1,0:T(8,128)}, u32[]{:S(2)}, u32[]{:S(2)}) collective-permute-start(f32[8,1536]{1,0:T(8,128)S(1)} %fusion), channel_id=1, source_target_pairs={{0,20},{1,21},{2,22},{3,23},{4,24},{5,25},{6,26},{7,27},{8,28},{9,... | collective-permute-start | bytes 147464
  1170.9 71.9 %collective-permute-start.30 = (f32[8,1536]{1,0:T(8,128)S(1)}, f32[8,1536]{1,0:T(8,128)}, u32[]{:S(2)}, u32[]{:S(2)}) collective-permute-start(f32[8,1536]{1,0:T(8,128)S(1)} %fusion), channel_id=1, source_target_pairs={{0,21},{1,22},{2,23},{3,24},{4,25},{5,26},{6,27},{7,28},{8,29},{9,... | collective-permute-start | bytes 147464
  1184.7 71.3 %collective-permute-start.31 = (f32[8,1536]{1,0:T(8,128)S(1)}, f32[8,1536]{1,0:T(8,128)}, u32[]{:S(2)}, u32[]{:S(2)}) collective-permute-start(f32[8,1536]{1,0:T(8,128)S(1)} %fusion), channel_id=1, source_target_pairs={{0,22},{1,23},{2,24},{3,25},{4,26},{5,27},{6,28},{7,29},{8,30},{9,... | collective-permute-start | bytes 147464
  1270.8 103.1 %collective-permute-start.37 = (f32[8,1536]{1,0:T(8,128)S(1)}, f32[8,1536]{1,0:T(8,128)}, u32[]{:S(2)}, u32[]{:S(2)}) collective-permute-start(f32[8,1536]{1,0:T(8,128)S(1)} %fusion), channel_id=1, source_target_pairs={{0,28},{1,29},{2,30},{3,31},{4,32},{5,33},{6,34},{7,35},{8,36},{9,... | collective-permute-start | bytes 147464
  1284.6 98.0 %collective-permute-start.38 = (f32[8,1536]{1,0:T(8,128)S(1)}, f32[8,1536]{1,0:T(8,128)}, u32[]{:S(2)}, u32[]{:S(2)}) collective-permute-start(f32[8,1536]{1,0:T(8,128)S(1)} %fusion), channel_id=1, source_target_pairs={{0,29},{1,30},{2,31},{3,32},{4,33},{5,34},{6,35},{7,36},{8,37},{9,... | collective-permute-start | bytes 147464
  1297.7 87.9 %collective-permute-start.39 = (f32[8,1536]{1,0:T(8,128)S(1)}, f32[8,1536]{1,0:T(8,128)}, u32[]{:S(2)}, u32[]{:S(2)}) collective-permute-start(f32[8,1536]{1,0:T(8,128)S(1)} %fusion), channel_id=1, source_target_pairs={{0,30},{1,31},{2,32},{3,33},{4,34},{5,35},{6,36},{7,37},{8,38},{9,... | collective-permute-start | bytes 147464
  1310.9 84.3 %collective-permute-start.40 = (f32[8,1536]{1,0:T(8,128)S(1)}, f32[8,1536]{1,0:T(8,128)}, u32[]{:S(2)}, u32[]{:S(2)}) collective-permute-start(f32[8,1536]{1,0:T(8,128)S(1)} %fusion), channel_id=1, source_target_pairs={{0,31},{1,32},{2,33},{3,34},{4,35},{5,36},{6,37},{7,38},{8,39},{9,... | collective-permute-start | bytes 147464
  1319.3 78.8 %collective-permute-start.41 = (f32[8,1536]{1,0:T(8,128)S(1)}, f32[8,1536]{1,0:T(8,128)}, u32[]{:S(2)}, u32[]{:S(2)}) collective-permute-start(f32[8,1536]{1,0:T(8,128)S(1)} %fusion), channel_id=1, source_target_pairs={{0,32},{1,33},{2,34},{3,35},{4,36},{5,37},{6,38},{7,39},{8,40},{9,... | collective-permute-start | bytes 147464
  1469.4 282.6 %collective-permute-start.8 = (bf16[2,256,1536]{1,2,0:T(8,128)(2,1)}, bf16[2,256,1536]{1,2,0:T(8,128)(2,1)}, u32[]{:S(2)}, u32[]{:S(2)}) collective-permute-start(bf16[2,256,1536]{1,2,0:T(8,128)(2,1)} %pad_maximum_fusion.1), channel_id=1, source_target_pairs={{1,0},{2,1},{3,2},{4,3},{5,4},{6,5},{7,6},{8,7},{9,8},{10,9},{11,1... | collective-permute-start | bytes 4718600 | tf_op jit(solution)/shard_map/ppermute | solution.py:31
  1471.8 281.9 %collective-permute-start.9 = (bf16[2,256,1536]{1,2,0:T(8,128)(2,1)}, bf16[2,256,1536]{1,2,0:T(8,128)(2,1)}, u32[]{:S(2)}, u32[]{:S(2)}) collective-permute-start(bf16[2,256,1536]{1,2,0:T(8,128)(2,1)} %pad_maximum_fusion.2), channel_id=1, source_target_pairs={{0,1},{1,2},{2,3},{3,4},{4,5},{5,6},{6,7},{7,8},{8,9},{9,10},{10,1... | collective-permute-start | bytes 4718600 | tf_op jit(solution)/shard_map/ppermute | solution.py:31
  1479.9 270.6 %all-reduce.7.cloned.1.call-start = ((), (), s32[]{:S(2)}) async-start(), calls=%async_computation.1 | async-start | bytes 393216 | tf_op jit(solution)/shard_map/psum | solution.py:12
  1479.9 171.4 %collective-permute-start.70 = (f32[8,1536]{1,0:T(8,128)S(1)}, f32[8,1536]{1,0:T(8,128)}, u32[]{:S(2)}, u32[]{:S(2)}) collective-permute-start(f32[8,1536]{1,0:T(8,128)S(1)} %fusion), channel_id=1, source_target_pairs={{0,61},{1,62},{2,63},{3,64},{4,65},{5,66},{6,67},{7,68},{8,69},{9,... | collective-permute-start | bytes 147464
  1482.1 169.2 %collective-permute-start.71 = (f32[8,1536]{1,0:T(8,128)S(1)}, f32[8,1536]{1,0:T(8,128)}, u32[]{:S(2)}, u32[]{:S(2)}) collective-permute-start(f32[8,1536]{1,0:T(8,128)S(1)} %fusion), channel_id=1, source_target_pairs={{0,62},{1,63},{2,64},{3,65},{4,66},{5,67},{6,68},{7,69},{8,70},{9,... | collective-permute-start | bytes 147464
  1484.0 167.3 %collective-permute-start.72 = (f32[8,1536]{1,0:T(8,128)S(1)}, f32[8,1536]{1,0:T(8,128)}, u32[]{:S(2)}, u32[]{:S(2)}) collective-permute-start(f32[8,1536]{1,0:T(8,128)S(1)} %fusion), channel_id=1, source_target_pairs={{0,63},{1,64},{2,65},{3,66},{4,67},{5,68},{6,69},{7,70},{8,71},{9,... | collective-permute-start | bytes 147464
  (184 other events, 11043.4 us)
Sparse Core Ops, SparseCore 0:
  1480.0 171.2 all-reduce.4
  1653.6 44.7 all-reduce.6
